TPU v7x, 32 devices: a whole 2x2x4 slice. The times are simulated.
32 devices in a mesh: wide: 8 (over y, x, core), narrow: 4 (over z).
Axes of the slice: x: 2, y: 2, z: 4, core: 2. Of those that a mesh axis runs over, the one named last changes fastest.
Arguments:
- tokens: bfloat16 [32, 576, 768], P(('wide', 'narrow')), may hold values from -6 to 6
- live_mask: int32 [32, 576], P(('wide', 'narrow')), may hold values from 0 to 1, as said below
- routes: int32 [32, 576, 2], P(('wide', 'narrow')), may hold values from 0 to 7, all different within a row
- priority: int32 [32, 576], P(('wide', 'narrow')), may hold values from 0 to 575, each once within a row
- cotangent: bfloat16 [32, 576, 768], P(('wide', 'narrow')), may hold values from -6 to 6
- first_gain: float32 [768], replicated, may hold values from 0.25 to 1.75
- first_shift: float32 [768], replicated, may hold values from -1.75 to 1.75
- query_weight: bfloat16 [768, 768], replicated, may hold values from -0.21875 to 0.21875
- query_bias: float32 [768], replicated, may hold values from -3 to 3
- key_weight: bfloat16 [768, 768], replicated, may hold values from -0.21875 to 0.21875
- value_weight: bfloat16 [768, 768], replicated, may hold values from -0.21875 to 0.21875
- value_bias: float32 [768], replicated, may hold values from -3 to 3
- out_weight: bfloat16 [768, 768], replicated, may hold values from -2.5 to 2.5
- out_bias: float32 [768], replicated, may hold values from -1.75 to 1.75
- second_gain: float32 [768], replicated, may hold values from 0.25 to 1.75
- second_shift: float32 [768], replicated, may hold values from -1.75 to 1.75
- router_weight: bfloat16 [768, 8], replicated, may hold values from -0.15625 to 0.15625
- expert_in: bfloat16 [8, 768, 3072], P('wide', None, 'narrow'), may hold values from -0.21875 to 0.21875
- expert_in_bias: bfloat16 [8, 3072], P('wide', 'narrow'), may hold values from -3 to 3
- expert_out: bfloat16 [8, 3072, 768], P('wide', 'narrow'), may hold values from -0.75 to 0.75
- expert_out_bias: float32 [8, 768], replicated, may hold values from -12 to 12
Outputs:
- mixed_out: bfloat16 [32, 576, 768], P(('wide', 'narrow'))
- tokens_grad: float32 [32, 576, 768], P(('wide', 'narrow'))
- first_gain_grad: float32 [768], replicated
- first_shift_grad: float32 [768], replicated
- query_weight_grad: float32 [768, 768], replicated
- query_bias_grad: float32 [768], replicated
- key_weight_grad: float32 [768, 768], replicated
- value_weight_grad: float32 [768, 768], replicated
- value_bias_grad: float32 [768], replicated
- out_weight_grad: float32 [768, 768], replicated
- out_bias_grad: float32 [768], replicated
- second_gain_grad: float32 [768], replicated
- second_shift_grad: float32 [768], replicated
- router_grad: float32 [768, 8], replicated
- expert_in_grad: float32 [8, 768, 3072], P('wide', None, 'narrow')
- expert_in_bias_grad: float32 [8, 3072], P('wide', 'narrow')
- expert_out_grad: float32 [8, 3072, 768], P('wide', 'narrow')
- expert_out_bias_grad: float32 [8, 768], replicated
Inputs may be any that keep to these rules, and one draw needn't show every extreme that they name: `live_mask`: in each row, 1 on a leading run of at least 432 patches and 0 after it. The two experts of a patch differ; routes of padded patches are not used. `priority`: each row holds every number of 0 to 575 once; a smaller number is served first.
All inputs are finite; a program needn't handle non-finite values.
Results may differ from a plain program's by a relative error of at most 0.02.
Values may be sent and summed in bfloat16 or wider, within the bound.
No kernel may reach another device: no remote copies, remote signals or barrier semaphores. Data moves between devices by JAX's collectives and lax.ppermute only.
A program may use at most 256 MiB of HBM per device.

v0:
```python
from functools import partial

import jax
import jax.numpy as jnp
from jax import lax
from jax.sharding import PartitionSpec as P

HEADS = 12
HEAD_DIM = 64


epsilon = 1e-06
highest = lax.Precision.HIGHEST


def layer_norm(source, gain_vec, shift_vec):
    average = jnp.mean(source, axis=-1, keepdims=True)
    centred = source - average
    variance = jnp.mean(centred * centred, axis=-1, keepdims=True)
    return centred * lax.rsqrt(variance + epsilon) * gain_vec + shift_vec


def slot_table(alive, route_pair, order_key, experts, capacity):
    earlier = (order_key[None, :] < order_key[:, None]).astype(jnp.bfloat16)
    columns = lax.broadcasted_iota(jnp.int32, (1, experts), 1)
    first_pick = ((route_pair[:, 0:1] == columns) & alive[:, None]).astype(jnp.float32)
    second = ((route_pair[:, 1:2] == columns) & alive[:, None]).astype(jnp.float32)
    before_first = jnp.dot(
        earlier, first_pick.astype(jnp.bfloat16), preferred_element_type=jnp.float32
    )
    place_first = jnp.sum(before_first * first_pick, axis=1)
    already = jnp.sum(first_pick, axis=0, keepdims=True)
    before_second = (
        jnp.dot(earlier, second.astype(jnp.bfloat16), preferred_element_type=jnp.float32) + already
    )
    place_second = jnp.sum(before_second * second, axis=1)
    slots = lax.broadcasted_iota(jnp.int32, (1, experts * capacity), 1)

    def one_table(route_col, position, onehot):
        kept_mask = alive & (position < capacity)
        target = route_col * capacity + position.astype(jnp.int32)
        spread = ((slots == target[:, None]) & kept_mask[:, None]).astype(jnp.bfloat16)
        return (spread, onehot * kept_mask[:, None].astype(jnp.float32))

    spread_first, first_kept = one_table(route_pair[:, 0], place_first, first_pick)
    spread_second, second_kept = one_table(route_pair[:, 1], place_second, second)
    return (first_pick, second, spread_first, spread_second, first_kept, second_kept)


def masked_scores(queries, key_rows, live_row, scaling):
    scores = (
        jnp.einsum("qhd,khd->hqk", queries, key_rows, preferred_element_type=jnp.float32) * scaling
    )
    return jnp.where(live_row[None, None, :] > 0, scores, -1e30)


def attend_forward(queries, key_rows, value_rows, live_row, scaling):
    scores = masked_scores(queries, key_rows, live_row, scaling)
    maximum = jnp.max(scores, axis=-1, keepdims=True)
    weights = jnp.exp(scores - maximum)
    summed_weights = jnp.sum(weights, axis=-1, keepdims=True)
    attention_probs = (weights / summed_weights).astype(jnp.bfloat16)
    mixed_heads = jnp.einsum(
        "hqk,khd->qhd", attention_probs, value_rows, preferred_element_type=jnp.float32
    )
    return (mixed_heads.astype(jnp.bfloat16), maximum + jnp.log(summed_weights))


def attend_backward(queries, key_rows, value_rows, live_row, log_total, mixed_grad, scaling):
    scores = masked_scores(queries, key_rows, live_row, scaling)
    attention_probs = jnp.exp(scores - log_total)
    prob_grad = jnp.einsum(
        "qhd,khd->hqk", mixed_grad, value_rows, preferred_element_type=jnp.float32
    )
    value_grad = jnp.einsum(
        "hqk,qhd->khd",
        attention_probs.astype(jnp.bfloat16),
        mixed_grad,
        preferred_element_type=jnp.float32,
    )
    score_grad = attention_probs * (
        prob_grad - jnp.sum(attention_probs * prob_grad, axis=-1, keepdims=True)
    )
    score_grad = score_grad.astype(jnp.bfloat16)
    query_grad = (
        jnp.einsum("hqk,khd->qhd", score_grad, key_rows, preferred_element_type=jnp.float32)
        * scaling
    )
    key_grad = (
        jnp.einsum("hqk,qhd->khd", score_grad, queries, preferred_element_type=jnp.float32)
        * scaling
    )
    return (
        query_grad.astype(jnp.bfloat16),
        key_grad.astype(jnp.bfloat16),
        value_grad.astype(jnp.bfloat16),
    )


def local(
    tokens,
    live_mask,
    routes,
    priority,
    cotangent,
    first_gain,
    first_shift,
    query_weight,
    query_bias,
    key_weight,
    value_weight,
    value_bias,
    out_weight,
    out_bias,
    second_gain,
    second_shift,
    router_weight,
    expert_in,
    expert_in_bias,
    expert_out,
    expert_out_bias,
):
    sequences, patches, features = tokens.shape
    patches_dev = sequences * patches
    experts = expert_out_bias.shape[0]
    capacity = max(2, (210 * patches_dev + 100 * experts - 1) // (100 * experts))
    scaling = HEAD_DIM ** (-0.5)
    head_shape = (sequences, patches, HEADS, HEAD_DIM)
    inputs = tokens.astype(jnp.float32).reshape(patches_dev, features)
    normed = layer_norm(inputs, first_gain, first_shift).astype(jnp.bfloat16)
    queries = (
        jnp.dot(normed, query_weight, preferred_element_type=jnp.float32) + query_bias
    ).astype(jnp.bfloat16)
    key_rows = jnp.dot(normed, key_weight, preferred_element_type=jnp.float32).astype(jnp.bfloat16)
    value_rows = (
        jnp.dot(normed, value_weight, preferred_element_type=jnp.float32) + value_bias
    ).astype(jnp.bfloat16)
    queries = queries.reshape(head_shape)
    key_rows = key_rows.reshape(head_shape)
    value_rows = value_rows.reshape(head_shape)

    def forward_member(member):
        return attend_forward(member[0], member[1], member[2], member[3], scaling)

    mixed_heads, log_total = lax.map(forward_member, (queries, key_rows, value_rows, live_mask))
    mixed_heads = mixed_heads.reshape(patches_dev, features)
    residual = (
        inputs + jnp.dot(mixed_heads, out_weight, preferred_element_type=jnp.float32) + out_bias
    )
    second_normed = layer_norm(residual, second_gain, second_shift).astype(jnp.bfloat16)
    logits = jnp.dot(second_normed, router_weight, preferred_element_type=jnp.float32)
    chance = jax.nn.softmax(logits, axis=-1)
    order_key = (
        priority * sequences + lax.broadcasted_iota(jnp.int32, (sequences, patches), 0)
    ).reshape(patches_dev)
    first_pick, second, spread_first, spread_second, first_kept, second_kept = slot_table(
        live_mask.reshape(patches_dev) > 0,
        routes.reshape(patches_dev, 2),
        order_key,
        experts,
        capacity,
    )
    spread = spread_first + spread_second
    buffers = jnp.einsum("ts,td->sd", spread, second_normed, preferred_element_type=jnp.float32)
    buffers = buffers.astype(jnp.bfloat16).reshape(experts, capacity, features)
    arrived = lax.all_to_all(buffers, "wide", split_axis=0, concat_axis=1, tiled=True)
    full_in, full_bias, full_out = (
        lax.all_gather(expert_in, "narrow", axis=2, tiled=True),
        lax.all_gather(expert_in_bias, "narrow", axis=1, tiled=True),
        lax.all_gather(expert_out, "narrow", axis=1, tiled=True),
    )
    before = jnp.einsum("erd,edf->erf", arrived, full_in, preferred_element_type=jnp.float32)
    before = before + full_bias.astype(jnp.float32)[:, None, :]
    hidden = jax.nn.gelu(before, approximate=True).astype(jnp.bfloat16)
    produced = jnp.einsum(
        "erf,efd->erd", hidden, full_out, preferred_element_type=jnp.float32
    ).astype(jnp.bfloat16)
    returned = lax.all_to_all(produced, "wide", split_axis=1, concat_axis=0, tiled=True).reshape(
        experts * capacity, features
    )
    picked_first = jnp.dot(spread_first, returned, preferred_element_type=jnp.float32)
    picked_first = picked_first + jnp.dot(first_kept, expert_out_bias, precision=highest)
    picked_second = jnp.dot(spread_second, returned, preferred_element_type=jnp.float32)
    picked_second = picked_second + jnp.dot(second_kept, expert_out_bias, precision=highest)
    gate_first = jnp.sum(chance * first_pick, axis=1, keepdims=True)
    gate_second = jnp.sum(chance * second, axis=1, keepdims=True)
    output = residual + gate_first * picked_first + gate_second * picked_second
    output = output.astype(jnp.bfloat16).reshape(sequences, patches, features)
    upstream = cotangent.astype(jnp.float32).reshape(patches_dev, features)
    gate_first_grad = jnp.sum(upstream * picked_first, axis=1, keepdims=True)
    gate_second_grad = jnp.sum(upstream * picked_second, axis=1, keepdims=True)
    weighted_first = gate_first * upstream
    weighted_second = gate_second * upstream
    slot_grad = jnp.einsum(
        "ts,td->sd",
        jnp.concatenate([spread_first, spread_second], axis=0),
        jnp.concatenate([weighted_first, weighted_second], axis=0).astype(jnp.bfloat16),
        preferred_element_type=jnp.float32,
    ).astype(jnp.bfloat16)
    out_bias_sum = jnp.dot(first_kept.T, weighted_first, precision=highest) + jnp.dot(
        second_kept.T, weighted_second, precision=highest
    )
    chance_grad = first_pick * gate_first_grad + second * gate_second_grad
    logit_grad = chance * (chance_grad - jnp.sum(chance * chance_grad, axis=1, keepdims=True))
    logit_grad = logit_grad.astype(jnp.bfloat16)
    router_sum = jnp.dot(second_normed.T, logit_grad, preferred_element_type=jnp.float32)
    second_normed_grad = jnp.dot(logit_grad, router_weight.T, preferred_element_type=jnp.float32)
    back_arrived = lax.all_to_all(
        slot_grad.reshape(experts, capacity, features),
        "wide",
        split_axis=0,
        concat_axis=1,
        tiled=True,
    )
    gelu_forward = partial(jax.nn.gelu, approximate=True)
    hidden_grad = jnp.einsum(
        "erd,efd->erf", back_arrived, full_out, preferred_element_type=jnp.float32
    )
    unused, gelu_back = jax.vjp(gelu_forward, before)
    before_grad = gelu_back(hidden_grad)[0].astype(jnp.bfloat16)
    out_full = jnp.einsum("erf,erd->efd", hidden, back_arrived, preferred_element_type=jnp.float32)
    in_full = jnp.einsum("erd,erf->edf", arrived, before_grad, preferred_element_type=jnp.float32)
    bias_full = jnp.sum(before_grad.astype(jnp.float32), axis=1)
    expert_in_grad, expert_in_bias_grad, expert_out_grad = (
        lax.psum_scatter(in_full, "narrow", scatter_dimension=2, tiled=True),
        lax.psum_scatter(bias_full, "narrow", scatter_dimension=1, tiled=True),
        lax.psum_scatter(out_full, "narrow", scatter_dimension=1, tiled=True),
    )
    input_grads = jnp.einsum(
        "erf,edf->erd", before_grad, full_in, preferred_element_type=jnp.float32
    ).astype(jnp.bfloat16)
    back_tokens = lax.all_to_all(
        input_grads, "wide", split_axis=1, concat_axis=0, tiled=True
    ).reshape(experts * capacity, features)
    second_normed_grad = second_normed_grad + jnp.dot(
        spread, back_tokens, preferred_element_type=jnp.float32
    )
    unused, second_back = jax.vjp(layer_norm, residual, second_gain, second_shift)
    residual_part, second_gain_grad, second_shift_grad = second_back(second_normed_grad)
    residual_grad = upstream + residual_part
    attended_grad = residual_grad.astype(jnp.bfloat16)
    out_bias_grad = jnp.sum(attended_grad.astype(jnp.float32), axis=0)
    out_weight_grad = jnp.dot(mixed_heads.T, attended_grad, preferred_element_type=jnp.float32)
    mixed_grad = jnp.dot(attended_grad, out_weight.T, preferred_element_type=jnp.float32).astype(
        jnp.bfloat16
    )

    def backward_member(member):
        return attend_backward(
            member[0], member[1], member[2], member[3], member[4], member[5], scaling
        )

    query_grad, key_grad, value_grad = lax.map(
        backward_member,
        (queries, key_rows, value_rows, live_mask, log_total, mixed_grad.reshape(head_shape)),
    )
    query_grad = query_grad.reshape(patches_dev, features)
    key_grad = key_grad.reshape(patches_dev, features)
    value_grad = value_grad.reshape(patches_dev, features)
    query_bias_grad = jnp.sum(query_grad.astype(jnp.float32), axis=0)
    value_bias_grad = jnp.sum(value_grad.astype(jnp.float32), axis=0)
    query_weight_grad = jnp.dot(normed.T, query_grad, preferred_element_type=jnp.float32)
    key_weight_grad = jnp.dot(normed.T, key_grad, preferred_element_type=jnp.float32)
    value_weight_grad = jnp.dot(normed.T, value_grad, preferred_element_type=jnp.float32)
    normed_grad = jnp.dot(query_grad, query_weight.T, preferred_element_type=jnp.float32)
    normed_grad = normed_grad + jnp.dot(key_grad, key_weight.T, preferred_element_type=jnp.float32)
    normed_grad = normed_grad + jnp.dot(
        value_grad, value_weight.T, preferred_element_type=jnp.float32
    )
    unused, first_back = jax.vjp(layer_norm, inputs, first_gain, first_shift)
    input_part, first_gain_grad, first_shift_grad = first_back(normed_grad)
    tokens_grad = (residual_grad + input_part).reshape(sequences, patches, features)
    summed = lax.psum(
        (
            first_gain_grad,
            first_shift_grad,
            query_weight_grad,
            query_bias_grad,
            key_weight_grad,
            value_weight_grad,
            value_bias_grad,
            out_weight_grad,
            out_bias_grad,
            second_gain_grad,
            second_shift_grad,
            router_sum,
            out_bias_sum,
        ),
        ("wide", "narrow"),
    )
    return (
        output,
        tokens_grad,
        summed[0],
        summed[1],
        summed[2],
        summed[3],
        summed[4],
        summed[5],
        summed[6],
        summed[7],
        summed[8],
        summed[9],
        summed[10],
        summed[11],
        expert_in_grad,
        expert_in_bias_grad,
        expert_out_grad,
        summed[12],
    )


def solution(mesh):
    return jax.shard_map(
        local,
        mesh=mesh,
        in_specs=(
            P(("wide", "narrow"), None, None),
            P(("wide", "narrow"), None),
            P(("wide", "narrow"), None, None),
            P(("wide", "narrow"), None),
            P(("wide", "narrow"), None, None),
            P(),
            P(),
            P(),
            P(),
            P(),
            P(),
            P(),
            P(),
            P(),
            P(),
            P(),
            P(),
            P("wide", None, "narrow"),
            P("wide", "narrow"),
            P("wide", "narrow", None),
            P(),
        ),
        out_specs=(
            P(("wide", "narrow"), None, None),
            P(("wide", "narrow"), None, None),
            P(),
            P(),
            P(),
            P(),
            P(),
            P(),
            P(),
            P(),
            P(),
            P(),
            P(),
            P(),
            P("wide", None, "narrow"),
            P("wide", "narrow"),
            P("wide", "narrow", None),
            P(),
        ),
        check_vma=False,
    )
```

profile of v0, /device:TPU:0, one launch (start us, length us, event | category | flops | bytes accessed | tf_op | source)
XLA Modules:
  0.0 1151.4 jit_solution(6082594205264992678)
XLA Ops:
  26.1 10.8 fusion.174
  45.6 9.5 fusion.82
  66.5 14.0 %all_gather.10 = bf16[1,3072]{1,0:T(2,128)(2,1)S(1)} all-gather(bf16[1,768]{1,0:T(2,128)(2,1)S(1)} %copy-done.44), channel_id=1, replica_groups=mesh['wide'=8,'narrow'=4] {'narrow'}, dimensions={1}, use_global_device_ids=true | all-gather | bytes 7680 | tf_op jit(solution)/shard_map/all_gather | solution.py:169
  80.6 10.2 all-to-all-done
  90.8 11.1 all-gather.3.cloned.1.call-done
  101.9 11.4 convolution_add_fusion
  113.4 78.0 %all-gather.5.cloned.1.call-done = bf16[1,3072,768]{2,1,0:T(8,128)(2,1)} async-done(((bf16[1,768,768]{2,1,0:T(8,128)(2,1)}), bf16[1,3072,768]{2,1,0:T(8,128)(2,1)}) %all-gather.5.cloned.1.call-update) | async-done | bytes 4718608 | tf_op jit(solution)/shard_map/all_gather | solution.py:170
  191.4 13.3 %fusion.25 = bf16[1,1216,768]{2,1,0:T(8,128)(2,1)S(1)} fusion(bf16[1,3072,768]{2,1,0:T(8,128)(2,1)} %all-gather.5.cloned.1.call-done, f32[1216,3072]{1,0:T(8,128)} %convolution_add_fusion), kind=kOutput, calls=%fused_computation.40 | convolution fusion | flops 5772361728 | bytes 21528576 | tf_op jit(solution)/shard_map/erf,efd->erd/dot_general | solution.py:175
  204.7 14.3 %copy.102 = bf16[1,1216,768]{2,0,1:T(2,128)(2,1)} copy(bf16[1,1216,768]{2,1,0:T(8,128)(2,1)S(1)} %fusion.25) | data formatting | bytes 3735552 | tf_op jit(solution)/shard_map/convert_element_type | solution.py:177
  219.6 13.2 %reduce.16 = bf16[1216,768]{1,0:T(8,128)(2,1)} reduce(bf16[1216,1,768]{2,1,0:T(2,128)(2,1)} %bitcast.179, bf16[]{:T(256)} %broadcast.329), dimensions={1}, to_apply=%bitcast.178.reduce_sub_computation | reduce | bytes 3735554
  246.1 21.5 %all-to-all-done.1 = bf16[8,2,58368]{2,1,0:T(2,128)(2,1)} async-done(((bf16[8,2,58368]{2,1,0:T(2,128)(2,1)}), bf16[8,2,58368]{2,1,0:T(2,128)(2,1)}, u32[]{:S(2)}, u32[]{:S(2)}) %all-to-all-start.1) | async-done | bytes 1867808 | tf_op jit(solution)/shard_map/all_to_all | solution.py:178
  288.5 27.0 %all_to_all.16 = bf16[8,152,768]{2,1,0:T(8,128)(2,1)S(1)} all-to-all(bf16[8,152,768]{2,1,0:T(8,128)(2,1)S(1)} %bitcast.200), channel_id=1, replica_groups=mesh['wide'=8,'narrow'=4] {'wide'}, dimensions={0} | all-to-all | bytes 3735552 | tf_op jit(solution)/shard_map/all_to_all | solution.py:208
  315.5 18.1 %convert_reduce_fusion = (f32[3072]{0:T(1024)S(1)}, bf16[1216,3072]{1,0:T(8,128)(2,1)S(1)}) fusion(f32[1216,3072]{1,0:T(8,128)} %convolution_add_fusion, bf16[1216,768]{1,0:T(8,128)(2,1)S(1)} %bitcast.197, bf16[1,3072,768]{2,1,0:T(8,128)(2,1)S(1)} %bitcast.212), kind=kOutput, calls=%fused_computation.16 | convolution fusion | flops 5819986944 | bytes 29011968 | tf_op jit(solution)/shard_map/erd,efd->erf/dot_general | solution.py:216
  339.7 14.3 %copy.101 = bf16[1,1216,768]{2,0,1:T(2,128)(2,1)} copy(bf16[1,1216,768]{2,1,0:T(8,128)(2,1)S(1)} %fusion.28) | data formatting | bytes 3735552 | tf_op jit(solution)/shard_map/convert_element_type | solution.py:231
  354.0 13.2 %reduce.17 = bf16[1216,768]{1,0:T(8,128)(2,1)} reduce(bf16[1216,1,768]{2,1,0:T(2,128)(2,1)} %bitcast.180, bf16[]{:T(256)} %broadcast.329), dimensions={1}, to_apply=%bitcast.177.reduce_sub_computation | reduce | bytes 3735554
  383.2 18.3 %all-to-all-done.3 = bf16[8,2,58368]{2,1,0:T(2,128)(2,1)} async-done(((bf16[8,2,58368]{2,1,0:T(2,128)(2,1)}), bf16[8,2,58368]{2,1,0:T(2,128)(2,1)}, u32[]{:S(2)}, u32[]{:S(2)}) %all-to-all-start.3) | async-done | bytes 1867808 | tf_op jit(solution)/shard_map/all_to_all | solution.py:232
  430.6 11.3 multiply_reduce_fusion
  441.9 12.5 %multiply_convert_fusion = bf16[12,576,576]{1,2,0:T(8,128)(2,1)S(1)} fusion(f32[12,576,576]{1,2,0:T(8,128)} %get-tuple-element.118, f32[12,576,576]{1,2,0:T(8,128)} %get-tuple-element.110, f32[12,576]{1,0:T(8,128)S(1)} %get-tuple-element.117, f32[12,576]{1,0:T(8,128)S(1)} %log_add_fusion), kind=kLoop, calls=%fused_computation.2 | loop fusion | flops 15925248 | bytes 39868416 | tf_op jit(solution)/shard_map/while/body/eval_jaxpr/convert_element_type | solution.py:84
  479.7 14.3 %convolution_bitcast_fusion = f32[1,3072,768]{2,1,0:T(8,128)} fusion(bf16[1216,768]{1,0:T(8,128)(2,1)} %bitcast.198, f32[1216,3072]{1,0:T(8,128)} %convolution_add_fusion), kind=kOutput, calls=%fused_computation.23 | convolution fusion | flops 5771427840 | bytes 26247168 | tf_op jit(solution)/shard_map/erf,erd->efd/dot_general | solution.py:221
  494.1 11.5 convolution_bitcast_fusion.1
  511.3 85.2 %all-reduce.5.cloned.1.call-done = (f32[768]{0:T(1024)}, f32[768]{0:T(1024)}, f32[768]{0:T(1024)}, f32[768]{0:T(1024)}, f32[768]{0:T(1024)}, /*index=5*/f32[768]...) async-done(((f32[768]{0:T(1024)}, f32[768]{0:T(1024)}, f32[768]{0:T(1024)}, f32[768]{0:T(1024)}, f32[768]{0:T(1024)}, /*index=5*/f32[768]{0:T(1024)}, ...) | async-done | bytes 70672 | tf_op jit(solution)/shard_map/psum | solution.py:273
  596.5 202.7 %all-reduce.7.cloned.1.call-done = (f32[768,768]{1,0:T(8,128)}, f32[768,768]{1,0:T(8,128)}, f32[768,768]{1,0:T(8,128)}, f32[768,768]{1,0:T(8,128)}) async-done(((f32[768,768]{1,0:T(8,128)}, f32[768,768]{1,0:T(8,128)}, f32[768,768]{1,0:T(8,128)}, f32[768,768]{1,0:T(8,128)}), (f32[768,768]{1,0:T(8,128)}, f32[768,768]{1,0:T(8,128)}, f32[768,768]{1,0:T(8,128)}, ...) | async-done | bytes 9437200 | tf_op jit(solution)/shard_map/psum | solution.py:273
  799.1 164.2 %reduce-scatter.8.cloned.1.call-done = f32[1,768,768]{2,1,0:T(8,128)} async-done(((f32[1,3072,768]{2,1,0:T(8,128)}), f32[1,768,768]{2,1,0:T(8,128)}) %reduce-scatter.8.cloned.1.call-update) | async-done | bytes 2359312 | tf_op jit(solution)/shard_map/reduce_scatter | solution.py:227
  963.3 165.1 %reduce-scatter.6.cloned.1.call-done = f32[1,768,768]{2,1,0:T(8,128)} async-done(((f32[1,768,3072]{2,1,0:T(8,128)}), f32[1,768,768]{2,1,0:T(8,128)}) %reduce-scatter.6.cloned.1.call-update) | async-done | bytes 2359312 | tf_op jit(solution)/shard_map/reduce_scatter | solution.py:225
  (233 shorter events, 171.4 us)
Async XLA Ops:
  7.2 14.6 %copy-start = (bf16[768,768]{1,0:T(8,128)(2,1)S(1)}, bf16[768,768]{1,0:T(8,128)(2,1)}, u32[]{:S(2)}) copy-start(bf16[768,768]{1,0:T(8,128)(2,1)} %param.31) | copy-start | bytes 3538948
  7.2 94.7 %all-gather.3.cloned.1.call-start = ((), (), s32[]{:S(2)}) async-start(), calls=%async_computation.7 | async-start | bytes 5898240 | tf_op jit(solution)/shard_map/all_gather | solution.py:168
  8.0 183.4 %all-gather.5.cloned.1.call-start = ((), (), s32[]{:S(2)}) async-start(), calls=%async_computation.8 | async-start | bytes 5898240 | tf_op jit(solution)/shard_map/all_gather | solution.py:170
  9.6 12.2 %copy-start.24 = (f32[576]{0:T(1024)}, f32[576]{0:T(1024)S(1)}, u32[]{:S(2)}) copy-start(f32[576]{0:T(1024)S(1)} %broadcast_multiply_fusion.1) | copy-start | bytes 6916
  10.7 11.1 copy-start.31
  15.9 10.2 copy-start.10
  36.9 8.7 copy-start.14
  45.6 9.5 copy-start.47
  45.6 9.5 copy-start.53
  61.2 29.6 %all-to-all-start = ((bf16[8,152,768]{2,1,0:T(8,128)(2,1)}), bf16[8,152,768]{2,1,0:T(8,128)(2,1)}, u32[]{:S(2)}, u32[]{:S(2)}) async-start(bf16[8,152,768]{2,1,0:T(8,128)(2,1)} %bitcast.199), calls=%async_computation | async-start | bytes 3735552 | tf_op jit(solution)/shard_map/all_to_all | solution.py:166
  238.5 29.1 %all-to-all-start.1 = ((bf16[8,2,58368]{2,1,0:T(2,128)(2,1)}), bf16[8,2,58368]{2,1,0:T(2,128)(2,1)}, u32[]{:S(2)}, u32[]{:S(2)}) async-start(bf16[8,2,58368]{2,1,0:T(2,128)(2,1)} %reshape.425), calls=%async_computation.1 | async-start | bytes 3735552 | tf_op jit(solution)/shard_map/all_to_all | solution.py:178
  284.5 31.0 %slice-start.2 = ((s8[4718592]{0:T(1024)(128)(4,1)}), s8[4194304]{0:T(1024)(128)(4,1)S(1)}, s32[]{:S(2)}) async-start(s8[4718592]{0:T(1024)(128)(4,1)} %bitcast.211), calls=%async_computation.16 | async-start | bytes 8388608
  285.8 29.7 %slice-start.3 = ((s8[4718592]{0:T(1024)(128)(4,1)}), s8[524288]{0:T(1024)(128)(4,1)S(1)}, s32[]{:S(2)}) async-start(s8[4718592]{0:T(1024)(128)(4,1)} %bitcast.211), calls=%async_computation.17 | async-start | bytes 1048576
  288.5 45.2 %slice-start = ((s8[4718592]{0:T(1024)(128)(4,1)}), s8[4194304]{0:T(1024)(128)(4,1)S(1)}, s32[]{:S(2)}) async-start(s8[4718592]{0:T(1024)(128)(4,1)} %bitcast.209), calls=%async_computation.14 | async-start | bytes 8388608
  315.5 18.1 %copy-start.20 = (bf16[8,152,768]{2,1,0:T(8,128)(2,1)}, bf16[8,152,768]{2,1,0:T(8,128)(2,1)S(1)}, u32[]{:S(2)}) copy-start(bf16[8,152,768]{2,1,0:T(8,128)(2,1)S(1)} %all_to_all.16) | copy-start | bytes 5603332
  315.5 18.2 %slice-start.1 = ((s8[4718592]{0:T(1024)(128)(4,1)}), s8[524288]{0:T(1024)(128)(4,1)S(1)}, s32[]{:S(2)}) async-start(s8[4718592]{0:T(1024)(128)(4,1)} %bitcast.209), calls=%async_computation.15 | async-start | bytes 1048576
  372.9 28.5 %all-to-all-start.3 = ((bf16[8,2,58368]{2,1,0:T(2,128)(2,1)}), bf16[8,2,58368]{2,1,0:T(2,128)(2,1)}, u32[]{:S(2)}, u32[]{:S(2)}) async-start(bf16[8,2,58368]{2,1,0:T(2,128)(2,1)} %reshape.427), calls=%async_computation.3 | async-start | bytes 3735552 | tf_op jit(solution)/shard_map/all_to_all | solution.py:232
  377.3 128.3 %reduce-scatter.10.cloned.1.call-start = ((), (), s32[]{:S(2)}) async-start(), calls=%async_computation.11 | async-start | bytes 1966080
  383.1 213.3 %all-reduce.5.cloned.1.call-start = ((), (), s32[]{:S(2)}) async-start(), calls=%async_computation.12 | async-start | bytes 155648 | tf_op jit(solution)/shard_map/psum | solution.py:273
  421.6 8.9 copy-start.15
  441.9 12.5 %copy-start.12 = (bf16[576,768]{0,1:T(8,128)(2,1)S(1)}, bf16[576,768]{0,1:T(8,128)(2,1)}, u32[]{:S(2)}) copy-start(bf16[576,768]{0,1:T(8,128)(2,1)} %copy.70) | copy-start | bytes 2654212
  475.6 323.5 %all-reduce.7.cloned.1.call-start = ((), (), s32[]{:S(2)}) async-start(), calls=%async_computation.13 | async-start | bytes 18874368 | tf_op jit(solution)/shard_map/psum | solution.py:273
  479.7 483.6 %reduce-scatter.8.cloned.1.call-start = ((), (), s32[]{:S(2)}) async-start(), calls=%async_computation.10 | async-start | bytes 11796480 | tf_op jit(solution)/shard_map/reduce_scatter | solution.py:227
  494.0 634.3 %reduce-scatter.6.cloned.1.call-start = ((), (), s32[]{:S(2)}) async-start(), calls=%async_computation.9 | async-start | bytes 11796480 | tf_op jit(solution)/shard_map/reduce_scatter | solution.py:225
  (48 other events, 108.6 us)
Sparse Core Ops, SparseCore 0:
  9.7 92.2 all-gather.2
  103.5 87.8 all-gather.4
  383.3 34.1 reduce-scatter.9
  475.8 120.6 all-reduce.4
  604.8 194.2 all-reduce.6
  801.9 161.3 reduce-scatter.7
  966.2 162.0 reduce-scatter.5
where the time goes:
time: 1160 us; the launch traced here: 1150 us
  waiting for transfers between devices  758 us (65%)
  matrix products  175 us (15%)
  local copies, waits for them, and re-layouts  87.4 us (8%)
  other arithmetic  60.1 us (5%)
  blocking collectives  41 us (4%)
  starting transfers between devices  15.2 us (1%)
  between operations  15.2 us (1%)
    psum x2, waiting for transfers between devices, local(): lax.psum((first_gain_grad, first_shift_grad, query_weight_grad, query_bia...  288 us
    reduce_scatter x1, waiting for transfers between devices, local(): lax.psum_scatter(in_full, 'narrow', scatter_dimension=2, tiled=True)  165 us
    reduce_scatter x1, waiting for transfers between devices, local(): lax.psum_scatter(out_full, 'narrow', scatter_dimension=1, tiled=True)  164 us
    all_gather x1, waiting for transfers between devices, local(): lax.all_gather(expert_out, 'narrow', axis=1, tiled=True)  78 us
    unnamed x144, local copies, waits for them, and re-layouts  49.6 us
    all_to_all x1, blocking collectives, local(): lax.all_to_all(slot_grad.reshape(experts, capacity, features), 'wide', sp...  27 us
    unnamed x5, other arithmetic  26.4 us
  transfers between devices with their start and end apart: 10, of which 9 were waited for; matrix products, arithmetic and copies ran while one was open for 15% of the time, Pallas kernels for 0%

commit v1 on v0

v1 whole, which is shorter than its diff:
```python
from functools import partial

import jax
import jax.numpy as jnp
from jax import lax
from jax.experimental import pallas as pl
from jax.experimental.pallas import tpu as pltpu
from jax.sharding import PartitionSpec as P

HEADS = 12
HEAD_DIM = 64


epsilon = 1e-06
highest = lax.Precision.HIGHEST


def layer_norm(source, gain_vec, shift_vec):
    average = jnp.mean(source, axis=-1, keepdims=True)
    centred = source - average
    variance = jnp.mean(centred * centred, axis=-1, keepdims=True)
    return centred * lax.rsqrt(variance + epsilon) * gain_vec + shift_vec


def masked_scores(queries, key_rows, live_row, scaling):
    scores = (
        jnp.einsum("qhd,khd->hqk", queries, key_rows, preferred_element_type=jnp.float32) * scaling
    )
    return jnp.where(live_row[None, None, :] > 0, scores, -1e30)


def attend_forward(queries, key_rows, value_rows, live_row, scaling):
    scores = masked_scores(queries, key_rows, live_row, scaling)
    maximum = jnp.max(scores, axis=-1, keepdims=True)
    weights = jnp.exp(scores - maximum)
    summed_weights = jnp.sum(weights, axis=-1, keepdims=True)
    attention_probs = (weights / summed_weights).astype(jnp.bfloat16)
    mixed_heads = jnp.einsum(
        "hqk,khd->qhd", attention_probs, value_rows, preferred_element_type=jnp.float32
    )
    return (mixed_heads.astype(jnp.bfloat16), maximum + jnp.log(summed_weights))


def attend_backward(queries, key_rows, value_rows, live_row, log_total, mixed_grad, scaling):
    scores = masked_scores(queries, key_rows, live_row, scaling)
    attention_probs = jnp.exp(scores - log_total)
    prob_grad = jnp.einsum(
        "qhd,khd->hqk", mixed_grad, value_rows, preferred_element_type=jnp.float32
    )
    value_grad = jnp.einsum(
        "hqk,qhd->khd",
        attention_probs.astype(jnp.bfloat16),
        mixed_grad,
        preferred_element_type=jnp.float32,
    )
    score_grad = attention_probs * (
        prob_grad - jnp.sum(attention_probs * prob_grad, axis=-1, keepdims=True)
    )
    score_grad = score_grad.astype(jnp.bfloat16)
    query_grad = (
        jnp.einsum("hqk,khd->qhd", score_grad, key_rows, preferred_element_type=jnp.float32)
        * scaling
    )
    key_grad = (
        jnp.einsum("hqk,qhd->khd", score_grad, queries, preferred_element_type=jnp.float32)
        * scaling
    )
    return (
        query_grad.astype(jnp.bfloat16),
        key_grad.astype(jnp.bfloat16),
        value_grad.astype(jnp.bfloat16),
    )


f32 = jnp.float32
bf16 = jnp.bfloat16
GELU_SCALE = 0.7978845608028654
GELU_CUBE = 0.044715
BIAS_ROWS = 16


def slot_columns(alive, route_pair, order_key, experts, capacity, padded, own):
    earlier = (order_key[None, :] < order_key[:, None]).astype(bf16)
    columns = lax.broadcasted_iota(jnp.int32, (1, experts), 1)
    first_pick = ((route_pair[:, 0:1] == columns) & alive[:, None]).astype(f32)
    second = ((route_pair[:, 1:2] == columns) & alive[:, None]).astype(f32)
    both = jnp.concatenate([first_pick, second], axis=1).astype(bf16)
    ahead = jnp.dot(earlier, both, preferred_element_type=f32)
    place_first = jnp.sum(ahead[:, :experts] * first_pick, axis=1)
    already = jnp.sum(first_pick, axis=0, keepdims=True)
    place_second = jnp.sum((ahead[:, experts:] + already) * second, axis=1)
    slots = lax.broadcasted_iota(jnp.int32, (1, experts * padded), 1)

    def one_table(route_col, position, onehot):
        kept_mask = alive & (position < capacity)
        target = jnp.where(kept_mask, (route_col ^ own) * padded + position.astype(jnp.int32), -1)
        spread = (slots == target[:, None]).astype(bf16)
        return (spread, onehot * kept_mask[:, None].astype(f32))

    spread_first, first_kept = one_table(route_pair[:, 0], place_first, first_pick)
    spread_second, second_kept = one_table(route_pair[:, 1], place_second, second)
    return (first_pick, second, spread_first, spread_second, first_kept, second_kept)


def dot_nt(a, b):
    return lax.dot_general(a, b, (((1,), (1,)), ((), ())), preferred_element_type=f32)


def dot_tn(a, b):
    return lax.dot_general(a, b, (((0,), (0,)), ((), ())), preferred_element_type=f32)


def expert_kernel(first, last, *refs):
    refs = list(refs)
    x_ref, g_ref, in_ref, out_ref = refs[:4]
    del refs[:4]
    if first:
        router_ref, pick_ref = refs[:2]
        del refs[:2]
    else:
        made_ref, back_ref = refs[:2]
        del refs[:2]
    if first:
        slot_ref = refs.pop(0)
    prod_ref, ig_ref, gin_ref, gout_ref, gin, gout, gbias = refs
    step = pl.program_id(0)
    width = x_ref.shape[1]

    @pl.when(step == 0)
    def _():
        gin[...] = jnp.zeros_like(gin)
        gout[...] = jnp.zeros_like(gout)
        gbias[...] = jnp.zeros_like(gbias)

    x = x_ref[...]
    if first:
        logits = jnp.dot(x, router_ref[...], preferred_element_type=f32) + pick_ref[0:1, :]
        weights = jnp.exp(logits - jnp.max(logits, axis=1, keepdims=True))
        own = jnp.sum(weights * pick_ref[1:2, :], axis=1, keepdims=True)
        gate = own / jnp.sum(weights, axis=1, keepdims=True)
        slot_grad = (gate * g_ref[...].astype(f32)).astype(bf16)
        slot_ref[...] = slot_grad
    else:
        slot_grad = g_ref[...]
    w_in = in_ref[0:width, :]
    bias = in_ref[width : width + BIAS_ROWS, :].astype(f32)[0:1, :]
    v = jnp.dot(x, w_in, preferred_element_type=f32) + bias
    square = v * v
    t = jnp.tanh(GELU_SCALE * v * (1.0 + GELU_CUBE * square))
    half = 0.5 * (1.0 + t)
    hidden = (v * half).astype(bf16)
    slope = half + 0.5 * v * (1.0 - t * t) * (GELU_SCALE * (1.0 + 3.0 * GELU_CUBE * square))
    made = jnp.dot(hidden, out_ref[...], preferred_element_type=f32)
    before_grad = dot_nt(slot_grad, out_ref[...]) * slope
    before_grad_b = before_grad.astype(bf16)
    back = dot_nt(before_grad_b, w_in)
    if not first:
        made = made + made_ref[...]
        back = back + back_ref[...]
    prod_ref[...] = made.astype(prod_ref.dtype)
    ig_ref[...] = back.astype(ig_ref.dtype)
    gin[...] += dot_tn(x, before_grad_b)
    gout[...] += dot_tn(hidden, slot_grad)
    gbias[0:1, :] += jnp.sum(before_grad_b.astype(f32), axis=0, keepdims=True)

    @pl.when(step == pl.num_programs(0) - 1)
    def _():
        gin_ref[0:width, :] = gin[...].astype(gin_ref.dtype)
        gout_ref[...] = gout[...].astype(gout_ref.dtype)
        gin_ref[width : width + BIAS_ROWS, :] = jnp.broadcast_to(
            gbias[0:1, :], (BIAS_ROWS, gbias.shape[1])
        ).astype(gin_ref.dtype)


def expert_step(first, last, grad_type, x, g, w_in, w_out, extra):
    rows, width = x.shape
    block = 256 if rows % 256 == 0 else 128
    steps = rows // block
    hid = w_out.shape[0]
    row_spec = pl.BlockSpec((block, width), lambda i: (i, 0))
    whole = lambda a: pl.BlockSpec(a.shape, lambda i: (0, 0))
    in_specs = [row_spec, row_spec, whole(w_in), whole(w_out)]
    outs = []
    specs = []
    if first:
        in_specs += [whole(extra[0]), whole(extra[1])]
        outs.append(jax.ShapeDtypeStruct((rows, width), bf16))
        specs.append(row_spec)
    else:
        in_specs += [row_spec, row_spec]
    acc_type = bf16 if last else f32
    outs += [jax.ShapeDtypeStruct((rows, width), acc_type)] * 2
    outs += [
        jax.ShapeDtypeStruct((width + BIAS_ROWS, hid), grad_type),
        jax.ShapeDtypeStruct((hid, width), grad_type),
    ]
    specs += [row_spec, row_spec]
    specs += [
        pl.BlockSpec((width + BIAS_ROWS, hid), lambda i: (0, 0)),
        pl.BlockSpec((hid, width), lambda i: (0, 0)),
    ]
    return pl.pallas_call(
        partial(expert_kernel, first, last),
        grid=(steps,),
        in_specs=in_specs,
        out_specs=specs,
        out_shape=outs,
        scratch_shapes=[
            pltpu.VMEM((width, hid), f32),
            pltpu.VMEM((hid, width), f32),
            pltpu.VMEM((8, hid), f32),
        ],
        compiler_params=pltpu.CompilerParams(
            vmem_limit_bytes=40 * 1024 * 1024, dimension_semantics=("arbitrary",)
        ),
        cost_estimate=pl.CostEstimate(
            flops=12 * rows * width * hid,
            bytes_accessed=20 * rows * width,
            transcendentals=rows * hid,
        ),
        name="expert_step",
    )(x, g, w_in, w_out, *extra)


def place_kernel(order_ref, src_ref, dst_ref):
    base = pl.program_id(0) * dst_ref.shape[0]
    for j in range(dst_ref.shape[0]):
        dst_ref[j] = src_ref[order_ref[base + j]].astype(f32)


def put_in_place(pieces, order, group):
    count, rows, width = pieces.shape
    return pl.pallas_call(
        place_kernel,
        grid_spec=pltpu.PrefetchScalarGridSpec(
            num_scalar_prefetch=1,
            grid=(count // group,),
            in_specs=[pl.BlockSpec((count, rows, width), lambda i, o: (0, 0, 0))],
            out_specs=pl.BlockSpec((group, rows, width), lambda i, o: (i, 0, 0)),
        ),
        out_shape=jax.ShapeDtypeStruct((count, rows, width), f32),
        compiler_params=pltpu.CompilerParams(
            vmem_limit_bytes=32 * 1024 * 1024, dimension_semantics=("arbitrary",)
        ),
        name="put_in_place",
    )(order, pieces)


class Links:
    def __init__(self, wide, narrow):
        self.wide, self.narrow = wide, narrow
        self.chips = wide // 2
        self.w = lax.axis_index("wide")
        self.z = lax.axis_index("narrow")

    def swap(self, x, k):
        return lax.ppermute(x, "wide", [(i, i ^ k) for i in range(self.wide)])

    def shift(self, x, k=1):
        n = self.narrow
        return lax.ppermute(x, "narrow", [(i, (i + k) % n) for i in range(n)])

    def exchange(self, blocks):
        got = [blocks[0:1]] + [self.swap(blocks[k : k + 1], k) for k in range(1, self.wide)]
        return jnp.concatenate(got, axis=0)

    def sum_all(self, x):
        rows, d = x.shape
        core, chip = self.w & 1, self.w >> 1
        pick = lambda a, i: lax.dynamic_index_in_dim(a, i, 0, keepdims=False)
        x = x.astype(bf16).reshape(2, rows // 2, d)
        y = pick(x, core).astype(f32) + self.swap(pick(x, 1 - core), 1).astype(f32)
        y = y.astype(bf16).reshape(self.chips, rows // self.wide, d)
        total = pick(y, chip).astype(f32)
        for k in range(1, self.chips):
            total = total + self.swap(pick(y, chip ^ k), 2 * k).astype(f32)
        n = self.narrow
        total = total.astype(bf16).reshape(n, rows // (self.wide * n), d)
        part = pick(total, self.z).astype(f32)
        for k in range(1, n):
            part = part + self.shift(pick(total, (self.z + k) % n), k).astype(f32)
        part = part.astype(bf16)
        pieces = jnp.stack([part] + [self.shift(part, k) for k in range(1, n)])
        pieces = jnp.stack([pieces] + [self.swap(pieces, 2 * k) for k in range(1, self.chips)])
        pieces = jnp.stack([pieces, self.swap(pieces, 1)])
        pieces = pieces.reshape((self.wide * n,) + part.shape)
        place = jnp.arange(self.wide * n, dtype=jnp.int32)
        c, ch, j = place // (self.chips * n), (place // n) % self.chips, place % n
        order = ((c ^ core) * self.chips + (ch ^ chip)) * n + (self.z - j) % n
        return put_in_place(pieces, order.astype(jnp.int32), n).reshape(rows, d)

    def sum_small(self, x):
        k = 1
        while k < self.wide:
            x = x + self.swap(x, k)
            k *= 2
        return x + sum(self.shift(x, k) for k in range(1, self.narrow))


def local(
    wide,
    narrow,
    tokens,
    live_mask,
    routes,
    priority,
    cotangent,
    first_gain,
    first_shift,
    query_weight,
    query_bias,
    key_weight,
    value_weight,
    value_bias,
    out_weight,
    out_bias,
    second_gain,
    second_shift,
    router_weight,
    expert_in,
    expert_in_bias,
    expert_out,
    expert_out_bias,
):
    links = Links(wide, narrow)
    sequences, patches, features = tokens.shape
    patches_dev = sequences * patches
    experts = expert_out_bias.shape[0]
    capacity = max(2, (210 * patches_dev + 100 * experts - 1) // (100 * experts))
    padded = (capacity + 15) // 16 * 16
    scaling = HEAD_DIM ** (-0.5)
    head_shape = (patches, HEADS, HEAD_DIM)

    bias_rows = jnp.broadcast_to(expert_in_bias, (BIAS_ROWS, expert_in_bias.shape[1]))
    weights_in = [jnp.concatenate([expert_in[0], bias_rows], axis=0)]
    weights_out = [expert_out[0]]
    for _ in range(1, narrow):
        weights_in.append(links.shift(weights_in[-1]))
        weights_out.append(links.shift(weights_out[-1]))

    order_key = (
        priority * sequences + lax.broadcasted_iota(jnp.int32, (sequences, patches), 0)
    ).reshape(patches_dev)
    first_pick, second, spread_first, spread_second, first_kept, second_kept = slot_columns(
        live_mask.reshape(patches_dev) > 0,
        routes.reshape(patches_dev, 2),
        order_key,
        experts,
        capacity,
        padded,
        links.w,
    )
    spread = spread_first + spread_second

    def to_slots(rows):
        return dot_tn(spread, rows).astype(bf16).reshape(experts, padded, features)

    upstream_b = cotangent.reshape(patches_dev, features)
    up_slots = links.exchange(to_slots(upstream_b)).reshape(experts * padded, features)

    inputs = tokens.astype(f32).reshape(patches_dev, features)
    normed = layer_norm(inputs, first_gain, first_shift).astype(bf16)
    queries = (jnp.dot(normed, query_weight, preferred_element_type=f32) + query_bias).astype(bf16)
    key_rows = jnp.dot(normed, key_weight, preferred_element_type=f32).astype(bf16)
    value_rows = (jnp.dot(normed, value_weight, preferred_element_type=f32) + value_bias).astype(
        bf16
    )
    queries = queries.reshape(head_shape)
    key_rows = key_rows.reshape(head_shape)
    value_rows = value_rows.reshape(head_shape)
    mixed_heads, log_total = attend_forward(queries, key_rows, value_rows, live_mask[0], scaling)
    mixed_heads = mixed_heads.reshape(patches_dev, features)
    residual = inputs + jnp.dot(mixed_heads, out_weight, preferred_element_type=f32) + out_bias
    second_normed = layer_norm(residual, second_gain, second_shift).astype(bf16)
    logits = jnp.dot(second_normed, router_weight, preferred_element_type=f32)
    chance = jax.nn.softmax(logits, axis=-1)

    arrived = links.exchange(to_slots(second_normed)).reshape(experts * padded, features)

    router_wide = jnp.pad(router_weight, ((0, 0), (0, 128 - experts)))
    lanes = jnp.arange(128)
    pick_rows = jnp.stack(
        [jnp.where(lanes < experts, 0.0, -1e30), (lanes == links.w).astype(f32)] + [jnp.zeros(128)] * 6
    ).astype(f32)

    grads = []
    for s in range(narrow):
        grad_type = bf16 if s == 1 else f32
        if s == 0:
            slot_grad, made, back, gin, gout = expert_step(
                True, narrow == 1, grad_type, arrived, up_slots, weights_in[0], weights_out[0],
                (router_wide, pick_rows),
            )
        else:
            made, back, gin, gout = expert_step(
                False, s == narrow - 1, grad_type, arrived, slot_grad, weights_in[s], weights_out[s],
                (made, back),
            )
        grads.append((gin, gout))

    def collect(i):
        moving = grads[1][i]
        for s in range(2, narrow):
            moving = (links.shift(moving).astype(f32) + grads[s][i]).astype(bf16)
        return links.shift(moving).astype(f32) + grads[0][i]

    in_sum, out_sum = collect(0), collect(1)
    expert_in_grad = in_sum[None, :features]
    expert_in_bias_grad = in_sum[features : features + 1]
    expert_out_grad = out_sum[None]

    gate_dots = jnp.sum(made.astype(f32) * up_slots.astype(f32), axis=1).reshape(experts, padded)
    dots_high = gate_dots.astype(bf16)
    dots_low = (gate_dots - dots_high.astype(f32)).astype(bf16)
    dot_rows = jnp.pad(jnp.stack([dots_high, dots_low], axis=1), ((0, 0), (0, 0), (0, features - padded)))
    back = back.reshape(experts, padded, features)
    back = jnp.concatenate(
        [back[:, :capacity], dot_rows, jnp.zeros((experts, padded - capacity - 2, features), bf16)], axis=1
    )
    back_tokens = links.exchange(back)
    returned = links.exchange(made.reshape(experts, padded, features)).reshape(
        experts * padded, features
    )

    upstream = upstream_b.astype(f32)
    gate_first = jnp.sum(chance * first_pick, axis=1, keepdims=True)
    gate_second = jnp.sum(chance * second, axis=1, keepdims=True)
    slot_dots = back_tokens[:, capacity, :padded].astype(f32) + back_tokens[
        :, capacity + 1, :padded
    ].astype(f32)
    slot_dots = slot_dots.reshape(1, experts * padded)
    bias_dots = jnp.dot(upstream, expert_out_bias.T, precision=highest)
    gate_first_grad = jnp.sum(spread_first * slot_dots, axis=1, keepdims=True) + jnp.sum(
        first_kept * bias_dots, axis=1, keepdims=True
    )
    gate_second_grad = jnp.sum(spread_second * slot_dots, axis=1, keepdims=True) + jnp.sum(
        second_kept * bias_dots, axis=1, keepdims=True
    )
    out_bias_sum = jnp.dot(
        (gate_first * first_kept + gate_second * second_kept).T, upstream, precision=highest
    )
    chance_grad = first_pick * gate_first_grad + second * gate_second_grad
    logit_grad = chance * (chance_grad - jnp.sum(chance * chance_grad, axis=1, keepdims=True))
    logit_grad = logit_grad.astype(bf16)
    router_sum = jnp.dot(second_normed.T, logit_grad, preferred_element_type=f32)
    second_normed_grad = jnp.dot(logit_grad, router_weight.T, preferred_element_type=f32)
    second_normed_grad = second_normed_grad + jnp.dot(
        spread, back_tokens.reshape(experts * padded, features), preferred_element_type=f32
    )
    unused, second_back = jax.vjp(layer_norm, residual, second_gain, second_shift)
    residual_part, second_gain_grad, second_shift_grad = second_back(second_normed_grad)
    residual_grad = upstream + residual_part
    attended_grad = residual_grad.astype(bf16)
    out_bias_grad = jnp.sum(attended_grad.astype(f32), axis=0)
    out_weight_grad = jnp.dot(mixed_heads.T, attended_grad, preferred_element_type=f32)
    mixed_grad = jnp.dot(attended_grad, out_weight.T, preferred_element_type=f32).astype(bf16)

    out_weight_total = links.sum_all(out_weight_grad)

    query_grad, key_grad, value_grad = attend_backward(
        queries, key_rows, value_rows, live_mask[0], log_total, mixed_grad.reshape(head_shape), scaling
    )
    query_grad = query_grad.reshape(patches_dev, features)
    key_grad = key_grad.reshape(patches_dev, features)
    value_grad = value_grad.reshape(patches_dev, features)
    query_bias_grad = jnp.sum(query_grad.astype(f32), axis=0)
    value_bias_grad = jnp.sum(value_grad.astype(f32), axis=0)
    projection_grads = jnp.concatenate(
        [
            jnp.dot(normed.T, query_grad, preferred_element_type=f32),
            jnp.dot(normed.T, key_grad, preferred_element_type=f32),
            jnp.dot(normed.T, value_grad, preferred_element_type=f32),
        ],
        axis=0,
    )
    projection_total = links.sum_all(projection_grads).reshape(3, features, features)
    normed_grad = dot_nt(query_grad, query_weight)
    normed_grad = normed_grad + dot_nt(key_grad, key_weight)
    normed_grad = normed_grad + dot_nt(value_grad, value_weight)
    unused, first_back = jax.vjp(layer_norm, inputs, first_gain, first_shift)
    input_part, first_gain_grad, first_shift_grad = first_back(normed_grad)
    tokens_grad = (residual_grad + input_part).reshape(sequences, patches, features)

    picked_first = jnp.dot(spread_first, returned, preferred_element_type=f32)
    picked_second = jnp.dot(spread_second, returned, preferred_element_type=f32)
    gated_bias = jnp.dot(
        gate_first * first_kept + gate_second * second_kept, expert_out_bias, precision=highest
    )
    output = residual + gate_first * picked_first + gate_second * picked_second + gated_bias
    output = output.astype(bf16).reshape(sequences, patches, features)

    vectors = jnp.stack(
        [first_gain_grad, first_shift_grad, query_bias_grad, value_bias_grad, out_bias_grad,
         second_gain_grad, second_shift_grad]
    )
    small = jnp.concatenate([vectors, jnp.zeros((1, features), f32), router_sum.T, out_bias_sum], axis=0)
    small = links.sum_small(small)
    return (
        output,
        tokens_grad,
        small[0],
        small[1],
        projection_total[0],
        small[2],
        projection_total[1],
        projection_total[2],
        small[3],
        out_weight_total,
        small[4],
        small[5],
        small[6],
        small[8 : 8 + experts].T,
        expert_in_grad,
        expert_in_bias_grad,
        expert_out_grad,
        small[8 + experts : 8 + 2 * experts],
    )


def solution(mesh):
    return jax.shard_map(
        partial(local, mesh.shape["wide"], mesh.shape["narrow"]),
        mesh=mesh,
        in_specs=(
            P(("wide", "narrow"), None, None),
            P(("wide", "narrow"), None),
            P(("wide", "narrow"), None, None),
            P(("wide", "narrow"), None),
            P(("wide", "narrow"), None, None),
            P(),
            P(),
            P(),
            P(),
            P(),
            P(),
            P(),
            P(),
            P(),
            P(),
            P(),
            P(),
            P("wide", None, "narrow"),
            P("wide", "narrow"),
            P("wide", "narrow", None),
            P(),
        ),
        out_specs=(
            P(("wide", "narrow"), None, None),
            P(("wide", "narrow"), None, None),
            P(),
            P(),
            P(),
            P(),
            P(),
            P(),
            P(),
            P(),
            P(),
            P(),
            P(),
            P(),
            P("wide", None, "narrow"),
            P("wide", "narrow"),
            P("wide", "narrow", None),
            P(),
        ),
        check_vma=False,
    )
```

time: 1160 us -> 609 us (0.53)
  waiting for transfers between devices: 758 us -> 242 us
  matrix products: 175 us -> 92.6 us
  starting transfers between devices: 15.2 us -> 79.6 us
  Pallas kernels: 0 us -> 64.3 us
  blocking collectives: 41 us -> 0 us
  local copies, waits for them, and re-layouts: 87.4 us -> 66.6 us
  between operations: 15.2 us -> 2.52 us
    reduce_scatter x2 -> x0, waiting for transfers between devices: 329 us -> none  [the longest x1 165 us: local(): lax.psum_scatter(in_full, 'narrow', scatter_dimension=2, tiled=True)]
    psum x2 -> x0, waiting for transfers between devices: 288 us -> none  [local(): lax.psum((first_gain_grad, first_shift_grad, query_weight_grad, query_bia...]
    ppermute x0 -> x74, waiting for transfers between devices: none -> 242 us  [the longest x27 171 us: shift(): return lax.ppermute(x, 'narrow', [(i, (i + k) % n) for i in range(n)])]
    all_gather x2 -> x0, waiting for transfers between devices: 89.2 us -> none  [the longest x1 78 us: local(): lax.all_gather(expert_out, 'narrow', axis=1, tiled=True)]
    dot_general x32 -> x24, matrix products: 130 us -> 45.6 us  [the longest x2 5.88 us: dot_tn(): lax.dot_general(a, b, (((0,), (0,)), ((), ())), preferred_element_type=f32)]
    ppermute x0 -> x74, starting transfers between devices: none -> 79.6 us  [the longest x47 46.2 us: swap(): return lax.ppermute(x, 'wide', [(i, i ^ k) for i in range(self.wide)])]
    pallas_call x0 -> x6, Pallas kernels: none -> 64.3 us  [the longest x4 59.5 us: expert_step(): pl.pallas_call(partial(expert_kernel, first, last), grid=(steps,), in_spe...]
    all_to_all x3 -> x0, waiting for transfers between devices: 49.9 us -> none  [the longest x1 21.5 us: local(): lax.all_to_all(produced, 'wide', split_axis=1, concat_axis=0, tiled=True)]
  transfers between devices with their start and end apart: 10 -> 74, of which waited for: 9 -> 31; matrix products, arithmetic and copies ran while one was open for 15% -> 31% of each run, Pallas kernels for 0% -> 10%
where the time goes in v1:
time: 609 us; the launch traced here: 602 us
  waiting for transfers between devices  242 us (40%)
  matrix products  92.6 us (15%)
  starting transfers between devices  79.6 us (13%)
  local copies, waits for them, and re-layouts  66.6 us (11%)
  Pallas kernels  64.3 us (11%)
  other arithmetic  54.1 us (9%)
    ppermute x27, waiting for transfers between devices, shift(): return lax.ppermute(x, 'narrow', [(i, (i + k) % n) for i in range(n)])  171 us
    ppermute x47, waiting for transfers between devices, swap(): return lax.ppermute(x, 'wide', [(i, i ^ k) for i in range(self.wide)])  70.7 us
    pallas_call x4, Pallas kernels, expert_step(): pl.pallas_call(partial(expert_kernel, first, last), grid=(steps,), in_spe...  59.5 us
    ppermute x47, starting transfers between devices, swap(): return lax.ppermute(x, 'wide', [(i, i ^ k) for i in range(self.wide)])  46.2 us
    ppermute x27, starting transfers between devices, shift(): return lax.ppermute(x, 'narrow', [(i, (i + k) % n) for i in range(n)])  33.4 us
    unnamed x200, local copies, waits for them, and re-layouts  30 us
    convert_element_type x1, other arithmetic, attend_backward(): score_grad = score_grad.astype(jnp.bfloat16)  12.3 us
  transfers between devices with their start and end apart: 74, of which 31 were waited for; matrix products, arithmetic and copies ran while one was open for 31% of the time, Pallas kernels for 10%

profile of v1, /device:TPU:0, one launch (start us, length us, event | category | flops | bytes accessed | tf_op | source)
XLA Modules:
  0.0 601.6 jit_solution(4375233684496402)
XLA Ops:
  30.1 11.0 %fusion.149 = (f32[12,576]{1,0:T(8,128)S(1)}, f32[12,576,576]{1,2,0:T(8,128)}) fusion(bf16[576,12,64]{0,2,1:T(8,128)(2,1)} %bitcast.299, bf16[576,12,64]{0,2,1:T(8,128)(2,1)} %bitcast.295, pred[576]{0:T(1024)(128)(4,1)S(1)} %fusion.119), kind=kOutput, calls=%fused_computation.328 | convolution fusion | flops 521544960 | bytes 17722944 | tf_op jit(solution)/shard_map/qhd,khd->hqk/dot_general | solution.py:27
  41.1 8.6 %fusion = f32[12,576]{1,0:T(8,128)S(1)} fusion(f32[12,576,576]{1,2,0:T(8,128)} %get-tuple-element.148, f32[12,576]{1,0:T(8,128)S(1)} %get-tuple-element.147), kind=kLoop, calls=%fused_computation.6 | loop fusion | flops 7955712 | bytes 15980544 | tf_op jit(solution)/shard_map/reduce_sum | solution.py:36
  49.7 9.8 %fusion.44 = bf16[12,64,576]{2,1,0:T(8,128)(2,1)S(1)} fusion(bf16[576,12,64]{0,2,1:T(8,128)(2,1)} %bitcast.303, f32[12,576,576]{1,2,0:T(8,128)} %get-tuple-element.148, f32[12,576]{1,0:T(8,128)S(1)} %fusion, f32[12,576]{1,0:T(8,128)S(1)} %get-tuple-element.147), kind=kOutput, calls=%fused_computation.93 | convolution fusion | flops 521994240 | bytes 17750016 | tf_op jit(solution)/shard_map/hqk,khd->qhd/dot_general | solution.py:38
  100.5 10.3 %collective-permute-done.4 = bf16[1,160,768]{2,1,0:T(8,128)(2,1)S(1)} collective-permute-done((bf16[1,160,768]{2,1,0:T(8,128)(2,1)S(1)}, bf16[1,160,768]{2,1,0:T(8,128)(2,1)S(1)}, u32[]{:S(2)}, u32[]{:S(2)}) %collective-permute-start.4) | collective-permute-done | bytes 245792 | tf_op jit(solution)/shard_map/ppermute | solution.py:257
  112.1 14.2 %expert_step.4 = (bf16[1280,768]{1,0:T(8,128)(2,1)S(1)}, f32[1280,768]{1,0:T(8,128)}, f32[1280,768]{1,0:T(8,128)}, f32[784,768]{1,0:T(8,128)S(1)}, f32[768,768]{1,0:T(8,128)S(1)}) custom-call(bf16[1280,768]{1,0:T(8,128)(2,1)S(1)} %bitcast.287, bf16[1280,768]{1,0:T(8,128)(2,1)S(1)} %bitcast.285, bf16[784,768]{1,0:T(8,128)(2,1)S(1)} %copy-done.9, ...), custom_call_target="tpu_custom_call" | custom-call | flops 9059696640 | bytes 19660800 | tf_op jit(solution)/shard_map/expert_step/pallas_call | solution.py:202
  129.2 5.5 collective-permute-done.17.refs_3_
  134.7 15.2 %expert_step.5 = (f32[1280,768]{1,0:T(8,128)S(1)}, f32[1280,768]{1,0:T(8,128)}, bf16[784,768]{1,0:T(8,128)(2,1)S(1)}, bf16[768,768]{1,0:T(8,128)(2,1)}) custom-call(bf16[1280,768]{1,0:T(8,128)(2,1)S(1)} %bitcast.288, bf16[1280,768]{1,0:T(8,128)(2,1)S(1)} %get-tuple-element.35.refs_1_, bf16[784,768]{1,0:T(8,128)(2,1)} %collective-permute-done.14.refs_2_, ...), custom_call_target="tpu_custom_call" | custom-call | flops 9059696640 | bytes 19660800 | tf_op jit(solution)/shard_map/expert_step/pallas_call | solution.py:202
  155.1 30.7 %collective-permute-done.18.refs_3_ = bf16[768,768]{1,0:T(8,128)(2,1)} collective-permute-done((bf16[768,768]{1,0:T(8,128)(2,1)}, bf16[768,768]{1,0:T(8,128)(2,1)}, u32[]{:S(2)}, u32[]{:S(2)}) %collective-permute-start.18) | collective-permute-done | bytes 1179680 | tf_op jit(solution)/shard_map/ppermute | solution.py:261
  190.4 15.1 %expert_step.6 = (f32[1280,768]{1,0:T(8,128)}, f32[1280,768]{1,0:T(8,128)}, f32[784,768]{1,0:T(8,128)S(1)}, f32[768,768]{1,0:T(8,128)S(1)}) custom-call(bf16[1280,768]{1,0:T(8,128)(2,1)S(1)} %bitcast.289, bf16[1280,768]{1,0:T(8,128)(2,1)S(1)} %copy-done.16, bf16[784,768]{1,0:T(8,128)(2,1)} %collective-permute-done.15.refs_2_, ...), custom_call_target="tpu_custom_call" | custom-call | flops 9059696640 | bytes 19660800 | tf_op jit(solution)/shard_map/expert_step/pallas_call | solution.py:202
  205.5 5.5 collective-permute-done.71
  213.7 23.1 %collective-permute-done.68 = bf16[784,768]{1,0:T(8,128)(2,1)} collective-permute-done((bf16[784,768]{1,0:T(8,128)(2,1)S(1)}, bf16[784,768]{1,0:T(8,128)(2,1)}, u32[]{:S(2)}, u32[]{:S(2)}) %collective-permute-start.68) | collective-permute-done | bytes 1204256 | tf_op jit(solution)/shard_map/ppermute | solution.py:261
  239.5 22.5 %collective-permute-done.19.refs_3_ = bf16[768,768]{1,0:T(8,128)(2,1)S(1)} collective-permute-done((bf16[768,768]{1,0:T(8,128)(2,1)}, bf16[768,768]{1,0:T(8,128)(2,1)S(1)}, u32[]{:S(2)}, u32[]{:S(2)}) %collective-permute-start.19) | collective-permute-done | bytes 1179680 | tf_op jit(solution)/shard_map/ppermute | solution.py:261
  262.0 25.8 %collective-permute-done.16.refs_2_ = bf16[784,768]{1,0:T(8,128)(2,1)S(1)} collective-permute-done((bf16[784,768]{1,0:T(8,128)(2,1)}, bf16[784,768]{1,0:T(8,128)(2,1)S(1)}, u32[]{:S(2)}, u32[]{:S(2)}) %collective-permute-start.16) | collective-permute-done | bytes 1204256 | tf_op jit(solution)/shard_map/ppermute | solution.py:261
  287.8 15.0 %expert_step.7 = (bf16[1280,768]{1,0:T(8,128)(2,1)S(1)}, bf16[1280,768]{1,0:T(8,128)(2,1)S(1)}, f32[784,768]{1,0:T(8,128)}, f32[768,768]{1,0:T(8,128)S(1)}) custom-call(bf16[1280,768]{1,0:T(8,128)(2,1)S(1)} %bitcast.290, bf16[1280,768]{1,0:T(8,128)(2,1)S(1)} %copy-done.16, bf16[784,768]{1,0:T(8,128)(2,1)S(1)} %collective-permute-done.16.refs_2_, ...), custom_call_target="tpu_custom_call" | custom-call | flops 9059696640 | bytes 19660800 | tf_op jit(solution)/shard_map/expert_step/pallas_call | solution.py:202
  316.0 22.4 %collective-permute-done.69 = bf16[784,768]{1,0:T(8,128)(2,1)} collective-permute-done((bf16[784,768]{1,0:T(8,128)(2,1)}, bf16[784,768]{1,0:T(8,128)(2,1)}, u32[]{:S(2)}, u32[]{:S(2)}) %collective-permute-start.69) | collective-permute-done | bytes 1204256 | tf_op jit(solution)/shard_map/ppermute | solution.py:261
  347.6 14.8 %collective-permute-done.30 = bf16[1,160,768]{2,1,0:T(8,128)(2,1)S(1)} collective-permute-done((bf16[1,160,768]{2,1,0:T(8,128)(2,1)S(1)}, bf16[1,160,768]{2,1,0:T(8,128)(2,1)S(1)}, u32[]{:S(2)}, u32[]{:S(2)}) %collective-permute-start.30) | collective-permute-done | bytes 245792 | tf_op jit(solution)/shard_map/ppermute | solution.py:257
  382.5 11.6 %multiply_reduce_fusion = (f32[12,576]{1,0:T(8,128)S(1)}, f32[12,576,576]{1,2,0:T(8,128)}) fusion(f32[12,576,576]{1,2,0:T(8,128)} %get-tuple-element.148, f32[12,576]{1,0:T(8,128)S(1)} %log_add_fusion, bf16[576,12,64]{0,2,1:T(8,128)(2,1)S(1)} %bitcast.297, bf16[576,12,64]{0,2,1:T(8,128)(2,1)} %bitcast.304), kind=kOutput, calls=%fused_computation.1 | convolution fusion | flops 521544960 | bytes 33675264 | tf_op jit(solution)/shard_map/qhd,khd->hqk/dot_general | solution.py:47
  394.1 12.3 %multiply_convert_fusion = bf16[12,576,576]{1,2,0:T(8,128)(2,1)S(1)} fusion(f32[12,576,576]{1,2,0:T(8,128)} %get-tuple-element.155, f32[12,576,576]{1,2,0:T(8,128)} %get-tuple-element.148, f32[12,576]{1,0:T(8,128)S(1)} %get-tuple-element.154, f32[12,576]{1,0:T(8,128)S(1)} %log_add_fusion), kind=kLoop, calls=%fused_computation | loop fusion | flops 15925248 | bytes 39868416 | tf_op jit(solution)/shard_map/convert_element_type | solution.py:59
  411.5 9.5 %convert_reduce_fusion.1 = (f32[12,64]{1,0:T(8,128)}, bf16[12,64,576]{2,1,0:T(8,128)(2,1)S(1)}) fusion(bf16[576,12,64]{0,2,1:T(8,128)(2,1)S(1)} %bitcast.298, f32[12,576,576]{1,2,0:T(8,128)} %get-tuple-element.148, f32[12,576]{1,0:T(8,128)S(1)} %log_add_fusion), kind=kOutput, calls=%fused_computation.51 | convolution fusion | flops 518896896 | bytes 17725440 | tf_op jit(solution)/shard_map/hqk,qhd->khd/dot_general | solution.py:50
  495.4 7.2 %collective-permute-done.42 = bf16[288,768]{1,0:T(8,128)(2,1)S(1)} collective-permute-done((bf16[288,768]{1,0:T(8,128)(2,1)S(1)}, bf16[288,768]{1,0:T(8,128)(2,1)S(1)}, u32[]{:S(2)}, u32[]{:S(2)}) %collective-permute-start.42) | collective-permute-done | bytes 442400 | tf_op jit(solution)/shard_map/ppermute | solution.py:257
  512.6 9.4 %collective-permute-done.44 = bf16[72,768]{1,0:T(8,128)(2,1)S(1)} collective-permute-done((bf16[72,768]{1,0:T(8,128)(2,1)S(1)}, bf16[72,768]{1,0:T(8,128)(2,1)S(1)}, u32[]{:S(2)}, u32[]{:S(2)}) %collective-permute-start.44) | collective-permute-done | bytes 110624 | tf_op jit(solution)/shard_map/ppermute | solution.py:261
  550.4 8.1 %collective-permute-done.50 = bf16[4,72,768]{2,1,0:T(8,128)(2,1)S(1)} collective-permute-done((bf16[4,72,768]{2,1,0:T(8,128)(2,1)S(1)}, bf16[4,72,768]{2,1,0:T(8,128)(2,1)S(1)}, u32[]{:S(2)}, u32[]{:S(2)}) %collective-permute-start.50) | collective-permute-done | bytes 442400 | tf_op jit(solution)/shard_map/ppermute | solution.py:257
  559.9 6.1 %collective-permute-done.51 = bf16[4,72,768]{2,1,0:T(8,128)(2,1)S(1)} collective-permute-done((bf16[4,72,768]{2,1,0:T(8,128)(2,1)S(1)}, bf16[4,72,768]{2,1,0:T(8,128)(2,1)S(1)}, u32[]{:S(2)}, u32[]{:S(2)}) %collective-permute-start.51) | collective-permute-done | bytes 442400 | tf_op jit(solution)/shard_map/ppermute | solution.py:257
  567.4 11.5 %collective-permute-done.61 = bf16[24,768]{1,0:T(8,128)(2,1)S(1)} collective-permute-done((bf16[24,768]{1,0:T(8,128)(2,1)S(1)}, bf16[24,768]{1,0:T(8,128)(2,1)S(1)}, u32[]{:S(2)}, u32[]{:S(2)}) %collective-permute-start.61) | collective-permute-done | bytes 36896 | tf_op jit(solution)/shard_map/ppermute | solution.py:261
  (472 shorter events, 273.7 us)
Async XLA Ops:
  9.0 62.7 %collective-permute-start.7 = (bf16[1,160,768]{2,1,0:T(8,128)(2,1)}, bf16[1,160,768]{2,1,0:T(8,128)(2,1)}, u32[]{:S(2)}, u32[]{:S(2)}) collective-permute-start(bf16[1,160,768]{2,1,0:T(8,128)(2,1)} %get-tuple-element.111), channel_id=1, source_target_pairs={{0,4},{4,0},{8,12},{12,8},{16,20},{20,16},{24,28},{28,24},{1,5},{5... | collective-permute-start | bytes 737288 | tf_op jit(solution)/shard_map/ppermute | solution.py:257
  9.5 65.8 %collective-permute-start.8 = (bf16[1,160,768]{2,1,0:T(8,128)(2,1)}, bf16[1,160,768]{2,1,0:T(8,128)(2,1)}, u32[]{:S(2)}, u32[]{:S(2)}) collective-permute-start(bf16[1,160,768]{2,1,0:T(8,128)(2,1)} %get-tuple-element.110), channel_id=1, source_target_pairs={{0,8},{4,12},{8,0},{12,4},{16,24},{20,28},{24,16},{28,20},{1,9},{5... | collective-permute-start | bytes 737288 | tf_op jit(solution)/shard_map/ppermute | solution.py:257
  12.1 64.5 %collective-permute-start.9 = (bf16[1,160,768]{2,1,0:T(8,128)(2,1)}, bf16[1,160,768]{2,1,0:T(8,128)(2,1)}, u32[]{:S(2)}, u32[]{:S(2)}) collective-permute-start(bf16[1,160,768]{2,1,0:T(8,128)(2,1)} %get-tuple-element.109), channel_id=1, source_target_pairs={{0,12},{4,8},{8,4},{12,0},{16,28},{20,24},{24,20},{28,16},{1,13},{... | collective-permute-start | bytes 737288 | tf_op jit(solution)/shard_map/ppermute | solution.py:257
  12.1 66.0 %collective-permute-start.10 = (bf16[1,160,768]{2,1,0:T(8,128)(2,1)}, bf16[1,160,768]{2,1,0:T(8,128)(2,1)}, u32[]{:S(2)}, u32[]{:S(2)}) collective-permute-start(bf16[1,160,768]{2,1,0:T(8,128)(2,1)} %get-tuple-element.108), channel_id=1, source_target_pairs={{0,16},{4,20},{8,24},{12,28},{16,0},{20,4},{24,8},{28,12},{1,17},{... | collective-permute-start | bytes 737288 | tf_op jit(solution)/shard_map/ppermute | solution.py:257
  13.9 67.0 %collective-permute-start.11 = (bf16[1,160,768]{2,1,0:T(8,128)(2,1)}, bf16[1,160,768]{2,1,0:T(8,128)(2,1)}, u32[]{:S(2)}, u32[]{:S(2)}) collective-permute-start(bf16[1,160,768]{2,1,0:T(8,128)(2,1)} %get-tuple-element.107), channel_id=1, source_target_pairs={{0,20},{4,16},{8,28},{12,24},{16,4},{20,0},{24,12},{28,8},{1,21},{... | collective-permute-start | bytes 737288 | tf_op jit(solution)/shard_map/ppermute | solution.py:257
  111.0 74.8 %collective-permute-start.15 = (bf16[784,768]{1,0:T(8,128)(2,1)}, bf16[784,768]{1,0:T(8,128)(2,1)}, u32[]{:S(2)}, u32[]{:S(2)}) collective-permute-start(bf16[784,768]{1,0:T(8,128)(2,1)} %collective-permute-done.14.refs_2_), channel_id=1, source_target_pairs={{0,1},{1,2},{2,3},{3,0},{4,5},{5,6},{6,7},{7,4},{8,9},{9,10},{10,1... | collective-permute-start | bytes 3612680 | tf_op jit(solution)/shard_map/ppermute | solution.py:261
  134.7 51.1 %collective-permute-start.18 = (bf16[768,768]{1,0:T(8,128)(2,1)}, bf16[768,768]{1,0:T(8,128)(2,1)}, u32[]{:S(2)}, u32[]{:S(2)}) collective-permute-start(bf16[768,768]{1,0:T(8,128)(2,1)} %collective-permute-done.17.refs_3_), channel_id=1, source_target_pairs={{0,1},{1,2},{2,3},{3,0},{4,5},{5,6},{6,7},{7,4},{8,9},{9,10},{10,1... | collective-permute-start | bytes 3538952 | tf_op jit(solution)/shard_map/ppermute | solution.py:261
  151.7 59.3 %collective-permute-start.71 = (bf16[768,768]{1,0:T(8,128)(2,1)}, bf16[768,768]{1,0:T(8,128)(2,1)}, u32[]{:S(2)}, u32[]{:S(2)}) collective-permute-start(bf16[768,768]{1,0:T(8,128)(2,1)} %get-tuple-element.48), channel_id=1, source_target_pairs={{0,1},{1,2},{2,3},{3,0},{4,5},{5,6},{6,7},{7,4},{8,9},{9,10},{10,1... | collective-permute-start | bytes 3538952 | tf_op jit(solution)/shard_map/ppermute | solution.py:261
  153.3 83.5 %collective-permute-start.68 = (bf16[784,768]{1,0:T(8,128)(2,1)S(1)}, bf16[784,768]{1,0:T(8,128)(2,1)}, u32[]{:S(2)}, u32[]{:S(2)}) collective-permute-start(bf16[784,768]{1,0:T(8,128)(2,1)S(1)} %get-tuple-element.44), channel_id=1, source_target_pairs={{0,1},{1,2},{2,3},{3,0},{4,5},{5,6},{6,7},{7,4},{8,9},{9,10},{10,1... | collective-permute-start | bytes 3612680 | tf_op jit(solution)/shard_map/ppermute | solution.py:261
  185.7 76.3 %collective-permute-start.19 = (bf16[768,768]{1,0:T(8,128)(2,1)}, bf16[768,768]{1,0:T(8,128)(2,1)S(1)}, u32[]{:S(2)}, u32[]{:S(2)}) collective-permute-start(bf16[768,768]{1,0:T(8,128)(2,1)} %collective-permute-done.18.refs_3_), channel_id=1, source_target_pairs={{0,1},{1,2},{2,3},{3,0},{4,5},{5,6},{6,7},{7,4},{8,9},{9,10},{10,1... | collective-permute-start | bytes 3538952 | tf_op jit(solution)/shard_map/ppermute | solution.py:261
  185.8 102.0 %collective-permute-start.16 = (bf16[784,768]{1,0:T(8,128)(2,1)}, bf16[784,768]{1,0:T(8,128)(2,1)S(1)}, u32[]{:S(2)}, u32[]{:S(2)}) collective-permute-start(bf16[784,768]{1,0:T(8,128)(2,1)} %collective-permute-done.15.refs_2_), channel_id=1, source_target_pairs={{0,1},{1,2},{2,3},{3,0},{4,5},{5,6},{6,7},{7,4},{8,9},{9,10},{10,1... | collective-permute-start | bytes 3612680 | tf_op jit(solution)/shard_map/ppermute | solution.py:261
  213.6 99.6 %collective-permute-start.72 = (bf16[768,768]{1,0:T(8,128)(2,1)}, bf16[768,768]{1,0:T(8,128)(2,1)}, u32[]{:S(2)}, u32[]{:S(2)}) collective-permute-start(bf16[768,768]{1,0:T(8,128)(2,1)} %add_convert_fusion.3), channel_id=1, source_target_pairs={{0,1},{1,2},{2,3},{3,0},{4,5},{5,6},{6,7},{7,4},{8,9},{9,10},{10,1... | collective-permute-start | bytes 3538952 | tf_op jit(solution)/shard_map/ppermute | solution.py:261
  239.4 99.0 %collective-permute-start.69 = (bf16[784,768]{1,0:T(8,128)(2,1)}, bf16[784,768]{1,0:T(8,128)(2,1)}, u32[]{:S(2)}, u32[]{:S(2)}) collective-permute-start(bf16[784,768]{1,0:T(8,128)(2,1)} %add_convert_fusion.1), channel_id=1, source_target_pairs={{0,1},{1,2},{2,3},{3,0},{4,5},{5,6},{6,7},{7,4},{8,9},{9,10},{10,1... | collective-permute-start | bytes 3612680 | tf_op jit(solution)/shard_map/ppermute | solution.py:261
  309.0 37.1 %collective-permute-start.28 = (bf16[1,160,768]{2,1,0:T(8,128)(2,1)S(1)}, bf16[1,160,768]{2,1,0:T(8,128)(2,1)S(1)}, u32[]{:S(2)}, u32[]{:S(2)}) collective-permute-start(bf16[1,160,768]{2,1,0:T(8,128)(2,1)S(1)} %get-tuple-element.102), channel_id=1, source_target_pairs={{0,8},{4,12},{8,0},{12,4},{16,24},{20,28},{24,16},{28,20},{1,9},{5... | collective-permute-start | bytes 737288 | tf_op jit(solution)/shard_map/ppermute | solution.py:257
  310.4 37.1 %collective-permute-start.29 = (bf16[1,160,768]{2,1,0:T(8,128)(2,1)S(1)}, bf16[1,160,768]{2,1,0:T(8,128)(2,1)S(1)}, u32[]{:S(2)}, u32[]{:S(2)}) collective-permute-start(bf16[1,160,768]{2,1,0:T(8,128)(2,1)S(1)} %get-tuple-element.101), channel_id=1, source_target_pairs={{0,12},{4,8},{8,4},{12,0},{16,28},{20,24},{24,20},{28,16},{1,13},{... | collective-permute-start | bytes 737288 | tf_op jit(solution)/shard_map/ppermute | solution.py:257
  347.5 88.2 %collective-permute-start.20 = (bf16[1,160,768]{2,1,0:T(8,128)(2,1)}, bf16[1,160,768]{2,1,0:T(8,128)(2,1)}, u32[]{:S(2)}, u32[]{:S(2)}) collective-permute-start(bf16[1,160,768]{2,1,0:T(8,128)(2,1)} %get-tuple-element.96), channel_id=1, source_target_pairs={{0,4},{4,0},{8,12},{12,8},{16,20},{20,16},{24,28},{28,24},{1,5},{5... | collective-permute-start | bytes 737288 | tf_op jit(solution)/shard_map/ppermute | solution.py:257
  362.4 76.2 %collective-permute-start.21 = (bf16[1,160,768]{2,1,0:T(8,128)(2,1)}, bf16[1,160,768]{2,1,0:T(8,128)(2,1)}, u32[]{:S(2)}, u32[]{:S(2)}) collective-permute-start(bf16[1,160,768]{2,1,0:T(8,128)(2,1)} %get-tuple-element.95), channel_id=1, source_target_pairs={{0,8},{4,12},{8,0},{12,4},{16,24},{20,28},{24,16},{28,20},{1,9},{5... | collective-permute-start | bytes 737288 | tf_op jit(solution)/shard_map/ppermute | solution.py:257
  364.9 77.1 %collective-permute-start.22 = (bf16[1,160,768]{2,1,0:T(8,128)(2,1)}, bf16[1,160,768]{2,1,0:T(8,128)(2,1)}, u32[]{:S(2)}, u32[]{:S(2)}) collective-permute-start(bf16[1,160,768]{2,1,0:T(8,128)(2,1)} %get-tuple-element.94), channel_id=1, source_target_pairs={{0,12},{4,8},{8,4},{12,0},{16,28},{20,24},{24,20},{28,16},{1,13},{... | collective-permute-start | bytes 737288 | tf_op jit(solution)/shard_map/ppermute | solution.py:257
  366.8 77.0 %collective-permute-start.23 = (bf16[1,160,768]{2,1,0:T(8,128)(2,1)}, bf16[1,160,768]{2,1,0:T(8,128)(2,1)}, u32[]{:S(2)}, u32[]{:S(2)}) collective-permute-start(bf16[1,160,768]{2,1,0:T(8,128)(2,1)} %get-tuple-element.93), channel_id=1, source_target_pairs={{0,16},{4,20},{8,24},{12,28},{16,0},{20,4},{24,8},{28,12},{1,17},{... | collective-permute-start | bytes 737288 | tf_op jit(solution)/shard_map/ppermute | solution.py:257
  368.4 89.7 %collective-permute-start.24 = (bf16[1,160,768]{2,1,0:T(8,128)(2,1)}, bf16[1,160,768]{2,1,0:T(8,128)(2,1)}, u32[]{:S(2)}, u32[]{:S(2)}) collective-permute-start(bf16[1,160,768]{2,1,0:T(8,128)(2,1)} %get-tuple-element.92), channel_id=1, source_target_pairs={{0,20},{4,16},{8,28},{12,24},{16,4},{20,0},{24,12},{28,8},{1,21},{... | collective-permute-start | bytes 737288 | tf_op jit(solution)/shard_map/ppermute | solution.py:257
  442.0 45.4 %collective-permute-start.54 = (bf16[384,768]{1,0:T(8,128)(2,1)S(1)}, bf16[384,768]{1,0:T(8,128)(2,1)}, u32[]{:S(2)}, u32[]{:S(2)}) collective-permute-start(bf16[384,768]{1,0:T(8,128)(2,1)S(1)} %dynamic-slice_bitcast_fusion.1), channel_id=1, source_target_pairs={{0,4},{4,0},{8,12},{12,8},{16,20},{20,16},{24,28},{28,24},{1,5},{5... | collective-permute-start | bytes 1769480 | tf_op jit(solution)/shard_map/ppermute | solution.py:257
  487.3 97.0 %collective-permute-start.73 = (bf16[768,768]{1,0:T(8,128)(2,1)S(1)}, bf16[768,768]{1,0:T(8,128)(2,1)S(1)}, u32[]{:S(2)}, u32[]{:S(2)}) collective-permute-start(bf16[768,768]{1,0:T(8,128)(2,1)S(1)} %copy-done.39), channel_id=1, source_target_pairs={{0,1},{1,2},{2,3},{3,0},{4,5},{5,6},{6,7},{7,4},{8,9},{9,10},{10,1... | collective-permute-start | bytes 3538952 | tf_op jit(solution)/shard_map/ppermute | solution.py:261
  487.3 42.5 %collective-permute-start.37 = (f32[24,768]{1,0:T(8,128)S(1)}, f32[24,768]{1,0:T(8,128)S(1)}, u32[]{:S(2)}, u32[]{:S(2)}) collective-permute-start(f32[24,768]{1,0:T(8,128)S(1)} %add.375), channel_id=1, source_target_pairs={{0,1},{1,2},{2,3},{3,0},{4,5},{5,6},{6,7},{7,4},{8,9},{9,10},{10,1... | collective-permute-start | bytes 221192 | tf_op jit(solution)/shard_map/ppermute | solution.py:261
  549.0 41.6 %collective-permute-start.70 = (bf16[784,768]{1,0:T(8,128)(2,1)S(1)}, bf16[784,768]{1,0:T(8,128)(2,1)S(1)}, u32[]{:S(2)}, u32[]{:S(2)}) collective-permute-start(bf16[784,768]{1,0:T(8,128)(2,1)S(1)} %copy-done.36), channel_id=1, source_target_pairs={{0,1},{1,2},{2,3},{3,0},{4,5},{5,6},{6,7},{7,4},{8,9},{9,10},{10,1... | collective-permute-start | bytes 3612680 | tf_op jit(solution)/shard_map/ppermute | solution.py:261
  (136 other events, 3289.7 us)
